TPU v7x, 128 devices: a whole 4x4x4 slice. The times are simulated.
128 devices in a mesh: wave: 32 (over z, x, core), lat: 4 (over y).
Axes of the slice: x: 4, y: 4, z: 4, core: 2. Of those that a mesh axis runs over, the one named last changes fastest.
Arguments:
- spectral: bfloat16 [2, 64, 2, 2048, 192], P(None, 'wave', None, 'lat'), may hold values from -0.29882812 to 0.29882812
- legendre: bfloat16 [64, 2, 2048, 4096], P('wave', None, None, 'lat'), may hold values from -0.09375 to 0.09375
- wavenumber: int32 [64], replicated, may hold values from 0 to 7999, as said below
Outputs:
- flux: bfloat16 [4, 2048, 512, 128], P('lat', 'wave')
Inputs may be any that keep to these rules, and one draw needn't show every extreme that they name: `wavenumber`: the entries come in pairs: entries 2 i and 2 i + 1 are m and 7999 - m with m <= 3999; all entries are distinct, and 0 and 7999 are always present.
All inputs are finite; a program needn't handle non-finite values.
Results may differ from a plain program's by a relative error of at most 0.0066.
Values may be sent and summed in bfloat16 or wider, within the bound.
A program may use at most 128 MiB of HBM per device.

v0:
```python
import math

import jax
import jax.numpy as jnp
from jax import lax
from jax.sharding import PartitionSpec as P

TRUNC = 7999
NLONW = 512


def fourier_table(wavenumber):
    period = 2 * TRUNC + 2
    column = jnp.arange(NLONW, dtype=jnp.int32)
    phase_index = wavenumber[None, :] * column[:, None] % period
    angles = phase_index.astype(jnp.float32) * (2.0 * math.pi / period)
    weight = jnp.where(wavenumber == 0, 1.0, 2.0).astype(jnp.float32)
    phase_table = jnp.stack([weight * jnp.cos(angles), -weight * jnp.sin(angles)], axis=2)
    return phase_table.astype(jnp.bfloat16)


def valid_slots(wavenumber, slot_count):
    slot_index = jnp.arange(slot_count, dtype=jnp.int32)
    parity = jnp.arange(2, dtype=jnp.int32)
    degree = wavenumber[:, None, None] + 2 * slot_index[None, None, :] + parity[None, :, None]
    return degree <= TRUNC


def field_products(grid_values, levels):
    vorticity = grid_values[..., :levels]
    return jnp.concatenate(
        [
            vorticity * grid_values[..., levels : 2 * levels],
            vorticity * grid_values[..., 2 * levels :],
        ],
        axis=-1,
    )


def shards(spectral, legendre, wavenumber):
    batches, own_count, _, _, columns = spectral.shape
    levels = columns // 6
    wave_id = lax.axis_index("wave")
    own_waves = lax.dynamic_slice_in_dim(wavenumber, wave_id * own_count, own_count)
    phase_table = fourier_table(wavenumber)
    results = []
    for batch_index in range(batches):
        shard_piece = lax.all_gather(spectral[batch_index], "lat", axis=2, tiled=True)
        slot_count = shard_piece.shape[2]
        live_slots = valid_slots(own_waves, slot_count)
        shard_piece = jnp.where(
            live_slots[:, :, :, None], shard_piece, jnp.zeros((), shard_piece.dtype)
        )
        partial_value = lax.dot_general(
            legendre,
            shard_piece,
            (((2,), (2,)), ((0, 1), (0, 1))),
            preferred_element_type=jnp.float32,
        )
        hemisphere = jnp.concatenate(
            [partial_value[:, 0] + partial_value[:, 1], partial_value[:, 0] - partial_value[:, 1]],
            axis=1,
        ).astype(jnp.bfloat16)
        owned_rows = lax.all_to_all(hemisphere, "wave", split_axis=1, concat_axis=0, tiled=True)
        wave_count, lat_count = (owned_rows.shape[0], owned_rows.shape[1])
        spectra = owned_rows.reshape(wave_count, lat_count, 2, 3 * levels)
        grid_values = jnp.einsum(
            "omr,mqrc->qoc", phase_table, spectra, preferred_element_type=jnp.float32
        )
        results.append(field_products(grid_values, levels))
    return jnp.concatenate(results, axis=2).astype(jnp.bfloat16)[None]


def solution(mesh):
    return jax.shard_map(
        shards,
        mesh=mesh,
        in_specs=(P(None, "wave", None, "lat", None), P("wave", None, None, "lat"), P()),
        out_specs=P("lat", "wave", None, None),
        check_vma=False,
    )
```

profile of v0, /device:TPU:1, one launch (start us, length us, event | category | flops | bytes accessed | tf_op | source)
XLA Modules:
  0.0 192.4 jit_solution(7850414925452892916)
XLA Ops:
  6.5 2.6 %fusion.34 = (bf16[1,2,2,512,192]{3,4,2,1,0:T(8,128)(2,1)}, bf16[1,2,2,512,192]{3,4,2,1,0:T(8,128)(2,1)}) fusion(bf16[2,2,2,512,192]{3,4,2,1,0:T(8,128)(2,1)} %param.3), kind=kLoop, calls=%fused_computation.58 | loop fusion | bytes 3145728 | tf_op jit(solution)/shard_map/slice | solution.py:48
  9.2 0.0 all-gather.5.cloned.1.call-start
  9.3 0.7 all-gather.5.cloned.1.call-update
  10.0 0.1 dynamic_slice.3
  10.1 0.1 broadcast_add_fusion
  10.2 41.9 %all-gather.7.cloned.1.call-done = bf16[1,2,2,2048,192]{3,4,2,1,0:T(8,128)(2,1)} async-done(((bf16[1,2,2,512,192]{3,4,2,1,0:T(8,128)(2,1)}), bf16[1,2,2,2048,192]{3,4,2,1,0:T(8,128)(2,1)}) %all-gather.7.cloned.1.call-update) | async-done | bytes 3145744 | tf_op jit(solution)/shard_map/all_gather | solution.py:48
  52.1 8.5 %fusion.15 = f32[2,2,1024,192]{2,3,1,0:T(8,128)S(1)} fusion(bf16[2,2,2048,1024]{3,2,1,0:T(8,128)(2,1)} %param.4, bf16[1,2,2,2048,192]{3,4,2,1,0:T(8,128)(2,1)} %all-gather.7.cloned.1.call-done, pred[2,2,2048]{2,1,0:T(4,128)(4,1)S(1)} %add_compare_fusion), kind=kOutput, calls=%fused_computation.24 | convolution fusion | flops 3222798336 | bytes 23076864 | tf_op jit(solution)/shard_map/dot_general | solution.py:54
  60.7 0.2 fusion.23
  60.9 0.2 fusion.21
  61.1 0.1 pad_maximum_fusion.2
  61.3 3.8 %copy.34 = bf16[2,2048,192]{2,0,1:T(2,128)(2,1)} copy(bf16[2,2048,192]{1,2,0:T(8,128)(2,1)S(1)} %pad_maximum_fusion.2) | data formatting | bytes 3145728 | tf_op jit(solution)/shard_map/concatenate | solution.py:60
  65.1 7.7 %all-to-all-start.1 = ((bf16[2,2048,192]{2,0,1:T(2,128)(2,1)}), bf16[2,2048,192]{2,0,1:T(2,128)(2,1)S(1)}, u32[]{:S(2)}, u32[]{:S(2)}) async-start(bf16[2,2048,192]{2,0,1:T(2,128)(2,1)} %copy.34), calls=%async_computation.1 | async-start | bytes 4194304 | tf_op jit(solution)/shard_map/all_to_all | solution.py:64
  72.8 20.7 %all-gather.5.cloned.1.call-done = bf16[1,2,2,2048,192]{3,4,2,1,0:T(8,128)(2,1)} async-done(((bf16[1,2,2,512,192]{3,4,2,1,0:T(8,128)(2,1)}), bf16[1,2,2,2048,192]{3,4,2,1,0:T(8,128)(2,1)}) %all-gather.5.cloned.1.call-update) | async-done | bytes 3145744 | tf_op jit(solution)/shard_map/all_gather | solution.py:48
  93.5 8.5 %fusion.14 = f32[2,2,1024,192]{2,3,1,0:T(8,128)S(1)} fusion(bf16[2,2,2048,1024]{3,2,1,0:T(8,128)(2,1)} %param.4, bf16[1,2,2,2048,192]{3,4,2,1,0:T(8,128)(2,1)} %all-gather.5.cloned.1.call-done, pred[2,2,2048]{2,1,0:T(4,128)(4,1)S(1)} %add_compare_fusion), kind=kOutput, calls=%fused_computation.23 | convolution fusion | flops 3222798336 | bytes 23076864 | tf_op jit(solution)/shard_map/dot_general | solution.py:54
  102.1 0.2 fusion.22
  102.3 0.2 fusion.20
  102.5 1.3 pad_maximum_fusion.1
  103.8 6.1 %copy.27 = bf16[2,2048,192]{2,0,1:T(2,128)(2,1)} copy(bf16[2,2048,192]{1,2,0:T(8,128)(2,1)} %pad_maximum_fusion.1) | data formatting | bytes 3145728 | tf_op jit(solution)/shard_map/concatenate | solution.py:60
  109.9 7.8 %all-to-all-start = ((bf16[2,2048,192]{2,0,1:T(2,128)(2,1)}), bf16[2,2048,192]{2,0,1:T(2,128)(2,1)}, u32[]{:S(2)}, u32[]{:S(2)}) async-start(bf16[2,2048,192]{2,0,1:T(2,128)(2,1)} %copy.27), calls=%async_computation | async-start | bytes 4194304 | tf_op jit(solution)/shard_map/all_to_all | solution.py:64
  117.7 0.6 multiply_convert_fusion.1
  118.3 0.3 copy.35
  118.6 1.5 copy.36
  120.1 3.0 %reshape.234 = bf16[64,64,2,96]{3,2,1,0:T(2,128)(2,1)S(1)} reshape(bf16[32,2,64,192]{3,2,1,0:T(8,128)(2,1)} %copy.36) | data formatting | bytes 3145728 | tf_op jit(solution)/shard_map/reshape | solution.py:66
  123.1 22.4 %all-to-all-done = bf16[2,2048,192]{2,0,1:T(2,128)(2,1)} async-done(((bf16[2,2048,192]{2,0,1:T(2,128)(2,1)}), bf16[2,2048,192]{2,0,1:T(2,128)(2,1)}, u32[]{:S(2)}, u32[]{:S(2)}) %all-to-all-start) | async-done | bytes 1572896 | tf_op jit(solution)/shard_map/all_to_all | solution.py:64
  145.5 1.9 copy.28
  147.4 1.5 copy.29
  148.8 4.3 %reshape.233 = bf16[64,64,2,96]{3,2,1,0:T(2,128)(2,1)} reshape(bf16[32,2,64,192]{3,2,1,0:T(8,128)(2,1)} %copy.29) | data formatting | bytes 3145728 | tf_op jit(solution)/shard_map/reshape | solution.py:66
  153.1 3.6 %convolution_bitcast_fusion.1 = f32[64,512,96]{1,2,0:T(8,128)S(1)} fusion(bf16[64,64,2,96]{3,2,1,0:T(2,128)(2,1)} %reshape.233, bf16[512,64,1]{0,1,2:T(8,128)(2,1)S(1)} %get-tuple-element.12, bf16[512,64,1]{0,1,2:T(8,128)(2,1)S(1)} %get-tuple-element.11), kind=kOutput, calls=%fused_computation.2 | convolution fusion | flops 805371904 | bytes 14286848 | tf_op jit(solution)/shard_map/omr,mqrc->qoc/dot_general | solution.py:67
  156.7 6.6 %convolution_bitcast_fusion = f32[64,512,96]{1,2,0:T(8,128)} fusion(bf16[64,64,2,96]{3,2,1,0:T(2,128)(2,1)S(1)} %reshape.234, bf16[512,64,1]{0,1,2:T(8,128)(2,1)S(1)} %get-tuple-element.12, bf16[512,64,1]{0,1,2:T(8,128)(2,1)S(1)} %get-tuple-element.11), kind=kOutput, calls=%fused_computation.1 | convolution fusion | flops 805371904 | bytes 14286848 | tf_op jit(solution)/shard_map/omr,mqrc->qoc/dot_general | solution.py:67
  163.3 6.6 %fusion.8 = (bf16[1,64,512,32]{2,3,1,0:T(8,128)(2,1)S(1)}, bf16[1,64,512,32]{2,3,1,0:T(8,128)(2,1)S(1)}, bf16[1,64,512,32]{2,3,1,0:T(8,128)(2,1)S(1)}, bf16[1,64,512,32]{2,3,1,0:T(8,128)(2,1)S(1)}) fusion(f32[64,512,96]{1,2,0:T(8,128)S(1)} %convolution_bitcast_fusion.1, f32[64,512,96]{1,2,0:T(8,128)} %convolution_bitcast_fusion), kind=kLoop, calls=%fused_computation.17 | loop fusion | flops 8388608 | bytes 33554432 | tf_op jit(solution)/shard_map/concatenate | solution.py:71
  169.9 3.8 %pad_maximum_fusion = bf16[1,64,512,128]{2,3,1,0:T(8,128)(2,1)} fusion(bf16[1,64,512,32]{2,3,1,0:T(8,128)(2,1)S(1)} %get-tuple-element.15, bf16[1,64,512,32]{2,3,1,0:T(8,128)(2,1)S(1)} %get-tuple-element.16, bf16[1,64,512,32]{2,3,1,0:T(8,128)(2,1)S(1)} %get-tuple-element.6, bf16[1,64,512,32]{2,3,1,0:T(8,128)(2,1)S(1)} %get-tuple-element.5), kind=kLoop, calls=%fused_computation | loop fusion | flops 33554432 | bytes 16777216 | tf_op jit(solution)/shard_map/concatenate | solution.py:71
  173.6 11.9 %copy.38 = bf16[1,64,512,128]{3,2,1,0:T(8,128)(2,1)} copy(bf16[1,64,512,128]{2,3,1,0:T(8,128)(2,1)} %pad_maximum_fusion) | data formatting | bytes 16777216 | tf_op jit(solution)/shard_map/concatenate | solution.py:71
  (8 shorter events, 0.1 us)
Async XLA Ops:
  6.5 3.4 %copy-start = (s32[64]{0:T(128)S(1)}, s32[64]{0:T(128)}, u32[]{:S(2)}) copy-start(s32[64]{0:T(128)} %param.5) | copy-start | bytes 772
  6.5 45.6 %all-gather.7.cloned.1.call-start = ((), (), s32[]{:S(2)}) async-start(), calls=%async_computation.3 | async-start | bytes 3932160 | tf_op jit(solution)/shard_map/all_gather | solution.py:48
  9.2 84.3 %all-gather.5.cloned.1.call-start = ((), (), s32[]{:S(2)}) async-start(), calls=%async_computation.2 | async-start | bytes 3932160 | tf_op jit(solution)/shard_map/all_gather | solution.py:48
  65.1 44.8 %all-to-all-start.1 = ((bf16[2,2048,192]{2,0,1:T(2,128)(2,1)}), bf16[2,2048,192]{2,0,1:T(2,128)(2,1)S(1)}, u32[]{:S(2)}, u32[]{:S(2)}) async-start(bf16[2,2048,192]{2,0,1:T(2,128)(2,1)} %copy.34), calls=%async_computation.1 | async-start | bytes 4194304 | tf_op jit(solution)/shard_map/all_to_all | solution.py:64
  109.9 35.6 %all-to-all-start = ((bf16[2,2048,192]{2,0,1:T(2,128)(2,1)}), bf16[2,2048,192]{2,0,1:T(2,128)(2,1)}, u32[]{:S(2)}, u32[]{:S(2)}) async-start(bf16[2,2048,192]{2,0,1:T(2,128)(2,1)} %copy.27), calls=%async_computation | async-start | bytes 4194304 | tf_op jit(solution)/shard_map/all_to_all | solution.py:64
Sparse Core Ops, SparseCore 0:
  9.3 42.7 all-gather.6
  53.8 39.7 all-gather.4
where the time goes:
time: 194 us; the launch traced here: 192 us
  waiting for transfers between devices  85.8 us (44%)
  local copies, waits for them, and re-layouts  36.9 us (19%)
  matrix products  27.3 us (14%)
  starting transfers between devices  15.5 us (8%)
  between operations  13.5 us (7%)
  other arithmetic  13.4 us (7%)
    all_gather x2, waiting for transfers between devices, shards(): lax.all_gather(spectral[batch_index], 'lat', axis=2, tiled=True)  62.7 us
    all_to_all x2, waiting for transfers between devices, shards(): lax.all_to_all(hemisphere, 'wave', split_axis=1, concat_axis=0, tiled=True)  22.4 us
    dot_general x2, matrix products, shards(): lax.dot_general(legendre, shard_piece, (((2,), (2,)), ((0, 1), (0, 1))),...  17.1 us
    all_to_all x2, starting transfers between devices, shards(): lax.all_to_all(hemisphere, 'wave', split_axis=1, concat_axis=0, tiled=True)  15.5 us
    concatenate x1, local copies, waits for them, and re-layouts, shards(): return jnp.concatenate(results, axis=2).astype(jnp.bfloat16)[None]  11.9 us
    concatenate x2, other arithmetic, shards(): return jnp.concatenate(results, axis=2).astype(jnp.bfloat16)[None]  10.3 us
    dot_general x2, matrix products, shards(): jnp.einsum('omr,mqrc->qoc', phase_table, spectra, preferred_element_type=...  10.2 us
    concatenate x2, local copies, waits for them, and re-layouts, shards(): jnp.concatenate([partial_value[:, 0] + partial_value[:, 1], partial_value...  9.9 us
  transfers between devices with their start and end apart: 4, of which 3 were waited for; matrix products, arithmetic and copies ran while one was open for 18% of the time, Pallas kernels for 0%

commit v1 on v0

v1 whole, which is shorter than its diff:
```python
import functools
import math

import jax
import jax.numpy as jnp
from jax import lax
from jax.experimental import pallas as pl
from jax.experimental.pallas import tpu as pltpu
from jax.sharding import PartitionSpec as P

TRUNC = 7999
NLONW = 512
MESH = pl.DeviceIdType.MESH
F32 = jnp.float32
BF16 = jnp.bfloat16
GROUP = 128


def fourier_table(wavenumber):
    period = 2 * TRUNC + 2
    column = jnp.arange(NLONW, dtype=jnp.int32)
    phase_index = wavenumber[None, :] * column[:, None] % period
    angles = phase_index.astype(F32) * (2.0 * math.pi / period)
    weight = jnp.where(wavenumber == 0, 1.0, 2.0).astype(F32)
    return (weight * jnp.cos(angles)).astype(BF16), (-weight * jnp.sin(angles)).astype(BF16)


def exchange_kernel(
    waves, wn_ref, spec_ref, leg_ref, out_ref,
    spec_v, xg, leg_v, sb,
    spec_sem, leg_sem, own_sem, gs_sem, gr_sem, as_sem, ar_sem,
):
    wave = lax.axis_index("wave")
    lat = lax.axis_index("lat")
    plus, minus = lax.rem(lat + 1, 4), lax.rem(lat + 3, 4)
    batches, slots, _, depth, columns = spec_ref.shape
    levels = columns // 6
    chunks = 3 * slots
    rows = out_ref.shape[2]
    band = leg_ref.shape[3]
    tile = min(256, band)

    def spec_copy(s):
        return pltpu.make_async_copy(spec_ref.at[:, s], spec_v.at[:, s], spec_sem.at[s])

    def leg_copy(s):
        return pltpu.make_async_copy(leg_ref.at[s], leg_v.at[s], leg_sem.at[s])

    for s in range(slots):
        spec_copy(s).start()
    for s in range(slots):
        leg_copy(s).start()

    barrier = pltpu.get_barrier_semaphore()
    for other in (plus, minus):
        pl.semaphore_signal(barrier, inc=1, device_id=(wave, other), device_id_type=MESH)

    def greet(i, carry):
        peer = lax.rem(wave + i, waves)
        pl.semaphore_signal(barrier, inc=1, device_id=(peer, lat), device_id_type=MESH)
        return carry

    lax.fori_loop(1, waves, greet, 0)

    def prepare(s):
        spec_copy(s).wait()
        first = wn_ref[wave * slots + s] + 2 * depth * lat
        slot_index = lax.broadcasted_iota(jnp.int32, (columns, depth), 1)
        for p in range(2):
            live = first + p + 2 * slot_index <= TRUNC
            for b in range(batches):
                turned = spec_v[b, s, p].astype(F32).T
                turned = jnp.where(live, turned, 0.0).astype(BF16)
                at = b * 2 * levels
                for r in range(2):
                    src = r * 3 * levels
                    xg[3 * s, 0, p, at + r * levels : at + (r + 1) * levels, :] = turned[
                        src : src + levels
                    ]
                    xg[3 * s + 1 + r, 0, p, at : at + 2 * levels, :] = turned[
                        src + levels : src + 3 * levels
                    ]

    def gather_copy(g, i):
        src, dst, p, to = (
            (0, 3, 0, plus), (0, 3, 1, plus), (0, 1, 0, minus), (0, 1, 1, minus),
            (3, 2, 0, plus), (1, 2, 1, minus),
        )[i]
        return pltpu.make_async_remote_copy(
            src_ref=xg.at[g, src, p],
            dst_ref=xg.at[g, dst, p],
            send_sem=gs_sem.at[g, i],
            recv_sem=gr_sem.at[g, i],
            device_id=(wave, to),
            device_id_type=MESH,
        )

    def start_own(g):
        for i in (0, 3, 1, 2):
            gather_copy(g, i).start()

    def self_copy(g):
        return pltpu.make_async_copy(sb.at[g, wave], out_ref.at[g, wave], own_sem.at[g])

    def all_of(g):
        peer = lax.rem(wave + 1, waves)
        return pltpu.make_async_remote_copy(
            src_ref=sb.at[g, pl.ds(0, waves - 1)],
            dst_ref=out_ref.at[g, pl.ds(0, waves - 1)],
            send_sem=as_sem.at[g],
            recv_sem=ar_sem.at[g],
            device_id=(peer, lat),
            device_id_type=MESH,
        )

    prepare(0)
    pl.semaphore_wait(barrier, waves + 1)
    start_own(0)
    start_own(1)
    for s in range(1, slots):
        prepare(s)

    def step(g, carry):
        s = g // 3
        gather_copy(g, 0).wait_recv()
        gather_copy(g, 4).start()
        gather_copy(g, 3).wait_recv()
        gather_copy(g, 5).start()

        @pl.when(g + 2 < chunks)
        def _():
            start_own(g + 2)

        for i in (1, 2, 4, 5):
            gather_copy(g, i).wait_recv()

        @pl.when(g == 3 * s)
        def _():
            leg_copy(s).wait()

        def columns_tile(n, inner):
            total = []
            for p in range(2):
                acc = None
                for j in range(4):
                    k0 = pl.multiple_of(lax.rem(lat + j, 4) * depth, depth)
                    poly = leg_v[s, p, pl.ds(k0, depth), pl.ds(pl.multiple_of(n * tile, tile), tile)]
                    part = jnp.dot(xg[g, j, p], poly, preferred_element_type=F32)
                    acc = part if acc is None else acc + part
                total.append(acc)
            per = tile // rows
            north = (total[0] + total[1]).T.astype(BF16)
            south = (total[0] - total[1]).T.astype(BF16)
            sb[g, pl.ds(n * per, per)] = north.reshape(per, rows, GROUP)
            sb[g, pl.ds(waves // 2 + n * per, per)] = south.reshape(per, rows, GROUP)
            return inner

        lax.fori_loop(0, band // tile, columns_tile, 0)

        def send(i, inner):
            peer = lax.rem(wave + i, waves)
            pltpu.make_async_remote_copy(
                src_ref=sb.at[g, peer],
                dst_ref=out_ref.at[g, wave],
                send_sem=as_sem.at[g],
                recv_sem=ar_sem.at[g],
                device_id=(peer, lat),
                device_id_type=MESH,
            ).start()
            return inner

        lax.fori_loop(1, waves, send, 0)
        self_copy(g).start()
        return carry

    lax.fori_loop(0, chunks, step, 0)

    def finish(g, carry):
        for i in range(6):
            gather_copy(g, i).wait_send()
        self_copy(g).wait()
        all_of(g).wait_send()
        all_of(g).wait_recv()
        return carry

    lax.fori_loop(0, chunks, finish, 0)


def synthesis_kernel(waves, block, table_ref, sums_ref, out_ref, wide):
    groups = sums_ref.shape[0]
    levels = GROUP // 4
    wide[...] = sums_ref[...].astype(F32).reshape(groups * waves * block, GROUP)
    lane = lax.broadcasted_iota(jnp.int32, (2 * waves, GROUP), 1)
    real_lane = (lane // levels) % 2 == 0

    def latitude(q, carry):
        def both(t):
            return jnp.concatenate(
                [wide[pl.ds((3 * s + t) * waves * block + q, waves, stride=block), :] for s in range(2)],
                axis=0,
            )

        vort = both(0)
        vort_real = jnp.where(real_lane, vort, pltpu.roll(vort, levels, 1))
        vort_imag = jnp.where(real_lane, pltpu.roll(vort, GROUP - levels, 1), vort)
        rhs = jnp.concatenate(
            [
                jnp.concatenate([vort_real, vort_imag], axis=0),
                jnp.concatenate([both(1), both(2)], axis=0),
            ],
            axis=1,
        ).astype(BF16)
        grid = jnp.dot(table_ref[...], rhs, preferred_element_type=F32)
        out_ref[q] = (grid[:, :GROUP] * grid[:, GROUP:]).astype(BF16)
        return carry

    lax.fori_loop(0, block, latitude, 0, unroll=2)


def shards(waves, spectral, legendre, wavenumber):
    batches, slots, _, depth, columns = spectral.shape
    bands = 4
    band = legendre.shape[3]
    rows = 2 * band // waves
    chunks = 3 * slots
    cosine, sine = fourier_table(wavenumber)
    table = jnp.stack([cosine, sine], axis=1)
    table = table.reshape(NLONW, 2, waves, slots).transpose(0, 1, 3, 2).reshape(NLONW, 2 * slots * waves)

    sums = pl.pallas_call(
        functools.partial(exchange_kernel, waves),
        out_shape=jax.ShapeDtypeStruct((chunks, waves, rows, GROUP), BF16),
        in_specs=[
            pl.BlockSpec(memory_space=pltpu.SMEM),
            pl.BlockSpec(memory_space=pl.ANY),
            pl.BlockSpec(memory_space=pl.ANY),
        ],
        out_specs=pl.BlockSpec(memory_space=pl.ANY),
        scratch_shapes=[
            pltpu.VMEM(spectral.shape, BF16),
            pltpu.VMEM((chunks, bands, 2, GROUP, depth), BF16),
            pltpu.VMEM(legendre.shape, BF16),
            pltpu.VMEM((chunks, waves, rows, GROUP), BF16),
            pltpu.SemaphoreType.DMA((slots,)),
            pltpu.SemaphoreType.DMA((slots,)),
            pltpu.SemaphoreType.DMA((chunks,)),
            pltpu.SemaphoreType.DMA((chunks, 6)),
            pltpu.SemaphoreType.DMA((chunks, 6)),
            pltpu.SemaphoreType.DMA((chunks,)),
            pltpu.SemaphoreType.DMA((chunks,)),
        ],
        compiler_params=pltpu.CompilerParams(
            collective_id=0, has_side_effects=True, vmem_limit_bytes=48 * 1024 * 1024
        ),
        name="gather_sum_exchange",
    )(wavenumber, spectral, legendre)

    block = 16
    flux = pl.pallas_call(
        functools.partial(synthesis_kernel, waves, block),
        grid=(rows // block,),
        out_shape=jax.ShapeDtypeStruct((rows, NLONW, GROUP), BF16),
        in_specs=[
            pl.BlockSpec(table.shape, lambda i: (0, 0)),
            pl.BlockSpec((chunks, waves, block, GROUP), lambda i: (0, 0, i, 0)),
        ],
        out_specs=pl.BlockSpec((block, NLONW, GROUP), lambda i: (i, 0, 0)),
        scratch_shapes=[pltpu.VMEM((chunks * waves * block, GROUP), F32)],
        compiler_params=pltpu.CompilerParams(vmem_limit_bytes=32 * 1024 * 1024),
        name="synthesis_product",
    )(table, sums)
    return flux[None]


def solution(mesh):
    return jax.shard_map(
        functools.partial(shards, mesh.shape["wave"]),
        mesh=mesh,
        in_specs=(P(None, "wave", None, "lat", None), P("wave", None, None, "lat"), P()),
        out_specs=P("lat", "wave", None, None),
        check_vma=False,
    )
```

time: 194 us -> 96.8 us (0.50)
  Pallas kernels: 0 us -> 91.2 us
  waiting for transfers between devices: 85.8 us -> 0 us
  local copies, waits for them, and re-layouts: 36.9 us -> 3.99 us
  matrix products: 27.3 us -> 0 us
  starting transfers between devices: 15.5 us -> 0 us
  between operations: 13.5 us -> 0.07 us
  other arithmetic: 13.4 us -> 1.38 us
    pallas_call x0 -> x2, Pallas kernels: none -> 91.2 us  [the longest x1 77.3 us: shards(): pl.pallas_call(functools.partial(exchange_kernel, waves), out_shape=jax.S...]
    all_gather x2 -> x0, waiting for transfers between devices: 62.7 us -> none  [shards(): lax.all_gather(spectral[batch_index], 'lat', axis=2, tiled=True)]
    dot_general x4 -> x0, matrix products: 27.3 us -> none  [the longest x2 17.1 us: shards(): lax.dot_general(legendre, shard_piece, (((2,), (2,)), ((0, 1), (0, 1))),...]
    all_to_all x2 -> x0, waiting for transfers between devices: 22.4 us -> none  [shards(): lax.all_to_all(hemisphere, 'wave', split_axis=1, concat_axis=0, tiled=True)]
    concatenate x3 -> x0, local copies, waits for them, and re-layouts: 21.8 us -> none  [the longest x1 11.9 us: shards(): return jnp.concatenate(results, axis=2).astype(jnp.bfloat16)[None]]
    all_to_all x2 -> x0, starting transfers between devices: 15.5 us -> none  [shards(): lax.all_to_all(hemisphere, 'wave', split_axis=1, concat_axis=0, tiled=True)]
    concatenate x4 -> x0, other arithmetic: 11.8 us -> none  [the longest x2 10.3 us: shards(): return jnp.concatenate(results, axis=2).astype(jnp.bfloat16)[None]]
    reshape x2 -> x1, local copies, waits for them, and re-layouts: 7.32 us -> 0.12 us  [shards(): table.reshape(NLONW, 2, waves, slots).transpose(0, 1, 3, 2)]
  transfers between devices with their start and end apart: 4 -> 0, of which waited for: 3 -> 0; matrix products, arithmetic and copies ran while one was open for 18% -> 0% of each run, Pallas kernels for 0% -> 0%
where the time goes in v1:
time: 96.8 us; the launch traced here: 96.6 us
  Pallas kernels  91.2 us (94%)
  local copies, waits for them, and re-layouts  3.99 us (4%)
  other arithmetic  1.38 us (1%)
    pallas_call x1, Pallas kernels, shards(): pl.pallas_call(functools.partial(exchange_kernel, waves), out_shape=jax.S...  77.3 us
    pallas_call x1, Pallas kernels, shards(): pl.pallas_call(functools.partial(synthesis_kernel, waves, block), grid=(r...  13.9 us
    unnamed x3, local copies, waits for them, and re-layouts  2.68 us

profile of v1, /device:TPU:1, one launch (start us, length us, event | category | flops | bytes accessed | tf_op | source)
XLA Modules:
  0.0 96.6 jit_solution(9322629276324987080)
XLA Ops:
  0.0 0.0 copy-start
  0.0 0.7 compare_select_fusion
  0.7 0.1 mul.83
  0.8 0.1 copy.8
  0.9 0.1 mul.92
  1.0 0.1 copy.10
  1.1 0.8 mul.85
  1.9 0.1 copy.9
  2.0 0.6 multiply_convert_fusion.1
  2.6 0.1 copy.12.table_ref
  2.7 2.7 %copy.11.spec_ref = bf16[2,2,2,512,192]{4,3,2,1,0:T(8,128)(2,1)S(1)} copy(bf16[2,2,2,512,192]{3,4,2,1,0:T(8,128)(2,1)} %param.3) | data formatting | bytes 3145728 | tf_op args[0]
  5.4 0.0 copy-done
  5.4 77.3 %gather_sum_exchange.1.sums_ref = bf16[6,32,64,128]{3,2,1,0:T(8,128)(2,1)S(1)} custom-call(s32[64]{0:T(128)S(1)} %copy-done, bf16[2,2,2,512,192]{4,3,2,1,0:T(8,128)(2,1)S(1)} %copy.11.spec_ref, bf16[2,2,2048,1024]{3,2,1,0:T(8,128)(2,1)} %leg_ref.1), custom_call_target="tpu_custom_call" | custom-call | tf_op jit(solution)/shard_map/gather_sum_exchange/pallas_call | solution.py:230
  82.7 13.9 %synthesis_product.1 = bf16[64,512,128]{2,1,0:T(8,128)(2,1)} custom-call(bf16[512,128]{1,0:T(8,128)(2,1)S(1)} %copy.12.table_ref, bf16[6,32,64,128]{3,2,1,0:T(8,128)(2,1)S(1)} %gather_sum_exchange.1.sums_ref), custom_call_target="tpu_custom_call" | custom-call | tf_op jit(solution)/shard_map/synthesis_product/pallas_call | solution.py:259
  (1 shorter events, 0.0 us)
Async XLA Ops:
  0.0 5.4 %copy-start = (s32[64]{0:T(128)S(1)}, s32[64]{0:T(128)}, u32[]{:S(2)}) copy-start(s32[64]{0:T(128)} %wn_ref.1) | copy-start | bytes 772

commit v2 on v1

v2 whole, which is shorter than its diff:
```python
import functools
import math

import jax
import jax.numpy as jnp
from jax import lax
from jax.experimental import pallas as pl
from jax.experimental.pallas import tpu as pltpu
from jax.sharding import PartitionSpec as P

TRUNC = 7999
NLONW = 512
PERIOD = 2 * TRUNC + 2
MESH = pl.DeviceIdType.MESH
F32 = jnp.float32
BF16 = jnp.bfloat16
BANDS = 4
GROUP = 128


def exchange_kernel(
    waves, wn_hbm, spec_ref, leg_ref, table_ref, held,
    xg, leg_v, sb, rv, wide,
    wn_ref, wn_sem, spec_sem, leg_sem, own_sem, gs_sem, gr_sem, as_sem, ar_sem,
):
    wave = lax.axis_index("wave")
    lat = lax.axis_index("lat")
    plus, minus = lax.rem(lat + 1, BANDS), lax.rem(lat + BANDS - 1, BANDS)
    batches, slots, _, columns, depth = spec_ref.shape
    levels = columns // 6
    chunks = 3 * slots
    rows = rv.shape[2]
    band = leg_ref.shape[3]
    tile = min(256, band)
    tiles = band // tile
    per = tile // rows
    half = waves // 2

    def spec_copies(s):
        copies = []
        for p in range(2):
            for b in range(batches):
                at = b * 2 * levels
                for r in range(2):
                    src = r * 3 * levels
                    copies.append((3 * s, p, at + r * levels, b, src, levels))
                    copies.append((3 * s + 1 + r, p, at, b, src + levels, 2 * levels))
        return [
            pltpu.make_async_copy(
                spec_ref.at[b, s, p, pl.ds(src, count)],
                xg.at[g, 0, p, pl.ds(dst, count)],
                spec_sem.at[s, n],
            )
            for n, (g, p, dst, b, src, count) in enumerate(copies)
        ]

    def leg_copy(s):
        return pltpu.make_async_copy(leg_ref.at[s], leg_v.at[s], leg_sem.at[s])

    numbers = pltpu.make_async_copy(wn_hbm, wn_ref, wn_sem)
    numbers.start()
    for s in range(slots):
        for copy in spec_copies(s):
            copy.start()

    barrier = pltpu.get_barrier_semaphore()
    for other in (plus, minus):
        pl.semaphore_signal(barrier, inc=1, device_id=(wave, other), device_id_type=MESH)

    def greet(i, carry):
        peer = lax.rem(wave + i, waves)
        pl.semaphore_signal(barrier, inc=1, device_id=(peer, lat), device_id_type=MESH)
        return carry

    lax.fori_loop(1, waves, greet, 0)
    for s in range(slots):
        leg_copy(s).start()

    def prepare(s):
        for copy in spec_copies(s):
            copy.wait()
        first = wn_ref[wave * slots + s] + 2 * depth * lat
        slot_index = lax.broadcasted_iota(jnp.int32, (GROUP, depth), 1)
        for p in range(2):
            live = first + p + 2 * slot_index <= TRUNC
            for t in range(3):
                g = 3 * s + t
                xg[g, 0, p] = jnp.where(live, xg[g, 0, p].astype(F32), 0.0).astype(BF16)

    def gather_copy(g, i):
        src, dst, p, to = (
            (0, 3, 0, plus), (0, 3, 1, plus), (0, 1, 0, minus), (0, 1, 1, minus),
            (3, 2, 0, plus), (1, 2, 1, minus),
        )[i]
        return pltpu.make_async_remote_copy(
            src_ref=xg.at[g, src, p],
            dst_ref=xg.at[g, dst, p],
            send_sem=gs_sem.at[g, i],
            recv_sem=gr_sem.at[g, i],
            device_id=(wave, to),
            device_id_type=MESH,
        )

    def start_own(g):
        for i in (0, 3, 1, 2):
            gather_copy(g, i).start()

    def self_copy(g):
        return pltpu.make_async_copy(sb.at[g, wave], rv.at[g, wave], own_sem.at[g])

    def all_of(g):
        peer = lax.rem(wave + 1, waves)
        return pltpu.make_async_remote_copy(
            src_ref=sb.at[g, pl.ds(0, waves - 1)],
            dst_ref=rv.at[g, pl.ds(0, waves - 1)],
            send_sem=as_sem.at[g],
            recv_sem=ar_sem.at[g],
            device_id=(peer, lat),
            device_id_type=MESH,
        )

    def make_table():
        lane = lax.broadcasted_iota(jnp.int32, (8, 2 * slots * waves), 1)
        slot = slots * lax.rem(lane, waves) + lax.rem(lane // waves, slots)
        number = jnp.zeros_like(lane)
        for n in range(slots * waves):
            number = jnp.where(slot == n, wn_ref[n], number)
        weight = jnp.where(number == 0, 1.0, 2.0).astype(F32)
        real = lane < slots * waves

        def block(i, carry):
            column = lax.broadcasted_iota(jnp.int32, lane.shape, 0)
            parts = []
            for n in range(2):
                product = number * (column + (16 * i + 8 * n))
                turns = jnp.floor(product.astype(F32) * (1.0 / PERIOD)).astype(jnp.int32)
                phase = product - turns * PERIOD
                phase = jnp.where(phase < 0, phase + PERIOD, phase)
                phase = jnp.where(phase >= PERIOD, phase - PERIOD, phase)
                angle = phase.astype(F32) * (2.0 * math.pi / PERIOD)
                parts.append(jnp.where(real, weight * jnp.cos(angle), -weight * jnp.sin(angle)))
            table_ref[pl.ds(pl.multiple_of(16 * i, 16), 16), :] = jnp.concatenate(parts, axis=0).astype(BF16)
            return carry

        lax.fori_loop(0, NLONW // 16, block, 0)

    def arrange(g):
        s = g // 3
        t = g - 3 * s
        all_of(g).wait_recv()
        self_copy(g).wait()
        wide[...] = rv[g].astype(F32).reshape(waves * rows, GROUP)
        lane = lax.broadcasted_iota(jnp.int32, (waves, GROUP), 1)
        real_lane = lax.rem(lane // levels, 2) == 0

        @pl.when(t == 0)
        def _():
            def latitude(q, carry):
                x = wide[pl.ds(q, waves, stride=rows), :]
                real = jnp.where(real_lane, x, pltpu.roll(x, levels, 1))
                imag = jnp.where(real_lane, pltpu.roll(x, GROUP - levels, 1), x)
                held[q, pl.ds(s * waves, waves), 0:GROUP] = real.astype(BF16)
                held[q, pl.ds((slots + s) * waves, waves), 0:GROUP] = imag.astype(BF16)
                return carry

            lax.fori_loop(0, rows, latitude, 0, unroll=8)

        @pl.when(t > 0)
        def _():
            r = t - 1

            def latitude(q, carry):
                x = wide[pl.ds(q, waves, stride=rows), :]
                held[q, pl.ds((r * slots + s) * waves, waves), GROUP : 2 * GROUP] = x.astype(BF16)
                return carry

            lax.fori_loop(0, rows, latitude, 0, unroll=8)

    numbers.wait()
    prepare(0)
    pl.semaphore_wait(barrier, waves + 1)
    start_own(0)
    for s in range(1, slots):
        prepare(s)
    make_table()

    def step(g, carry):
        s = g // 3
        gather_copy(g, 0).wait_recv()
        gather_copy(g, 4).start()
        gather_copy(g, 3).wait_recv()
        gather_copy(g, 5).start()

        @pl.when(g + 1 < chunks)
        def _():
            start_own(g + 1)

        @pl.when(g >= 2)
        def _():
            arrange(g - 2)

        for i in (1, 2, 4, 5):
            gather_copy(g, i).wait_recv()

        @pl.when(g == 3 * s)
        def _():
            leg_copy(s).wait()

        def columns_tile(turn, inner):
            n = lax.rem(turn + wave, tiles)
            total = []
            for p in range(2):
                acc = None
                for j in range(BANDS):
                    k0 = pl.multiple_of(lax.rem(lat + j, BANDS) * depth, depth)
                    poly = leg_v[s, p, pl.ds(k0, depth), pl.ds(pl.multiple_of(n * tile, tile), tile)]
                    part = jnp.dot(xg[g, j, p], poly, preferred_element_type=F32)
                    acc = part if acc is None else acc + part
                total.append(acc)
            north = (total[0] + total[1]).T.astype(BF16)
            south = (total[0] - total[1]).T.astype(BF16)
            sb[g, pl.ds(n * per, per)] = north.reshape(per, rows, GROUP)
            sb[g, pl.ds(half + n * per, per)] = south.reshape(per, rows, GROUP)

            def send(i, after):
                peer = n * per + lax.rem(i, per) + half * (i // per)

                @pl.when(peer != wave)
                def _():
                    pltpu.make_async_remote_copy(
                        src_ref=sb.at[g, peer],
                        dst_ref=rv.at[g, wave],
                        send_sem=as_sem.at[g],
                        recv_sem=ar_sem.at[g],
                        device_id=(peer, lat),
                        device_id_type=MESH,
                    ).start()

                return after

            lax.fori_loop(0, 2 * per, send, 0)
            return inner

        lax.fori_loop(0, tiles, columns_tile, 0)
        self_copy(g).start()
        return carry

    lax.fori_loop(0, chunks, step, 0)
    for g in range(chunks - 2, chunks):
        arrange(g)

    def finish(g, carry):
        for i in range(6):
            gather_copy(g, i).wait_send()
        all_of(g).wait_send()
        return carry

    lax.fori_loop(0, chunks, finish, 0)


def synthesis_kernel(block, table_ref, rhs_ref, out_ref):
    first = pl.program_id(0) * block
    for q in range(block):
        grid = jnp.dot(table_ref[...], rhs_ref[first + q], preferred_element_type=F32)
        out_ref[q] = (grid[:, :GROUP] * grid[:, GROUP:]).astype(BF16)


def shards(waves, spectral, legendre, wavenumber):
    spectral = jnp.swapaxes(spectral, 3, 4)
    slots = spectral.shape[1]
    depth = spectral.shape[4]
    rows = 2 * legendre.shape[3] // waves
    chunks = 3 * slots
    inner = 2 * slots * waves

    table, rhs = pl.pallas_call(
        functools.partial(exchange_kernel, waves),
        out_shape=[
            jax.ShapeDtypeStruct((NLONW, inner), BF16),
            jax.ShapeDtypeStruct((rows, inner, 2 * GROUP), BF16),
        ],
        in_specs=[
            pl.BlockSpec(memory_space=pl.ANY),
            pl.BlockSpec(memory_space=pl.ANY),
            pl.BlockSpec(memory_space=pl.ANY),
        ],
        out_specs=[pl.BlockSpec(memory_space=pltpu.VMEM)] * 2,
        scratch_shapes=[
            pltpu.VMEM((chunks, BANDS, 2, GROUP, depth), BF16),
            pltpu.VMEM(legendre.shape, BF16),
            pltpu.VMEM((chunks, waves, rows, GROUP), BF16),
            pltpu.VMEM((chunks, waves, rows, GROUP), BF16),
            pltpu.VMEM((waves * rows, GROUP), F32),
            pltpu.SMEM((slots * waves,), jnp.int32),
            pltpu.SemaphoreType.DMA,
            pltpu.SemaphoreType.DMA((slots, 16)),
            pltpu.SemaphoreType.DMA((slots,)),
            pltpu.SemaphoreType.DMA((chunks,)),
            pltpu.SemaphoreType.DMA((chunks, 6)),
            pltpu.SemaphoreType.DMA((chunks, 6)),
            pltpu.SemaphoreType.DMA((chunks,)),
            pltpu.SemaphoreType.DMA((chunks,)),
        ],
        compiler_params=pltpu.CompilerParams(
            collective_id=0, has_side_effects=True, vmem_limit_bytes=42 * 1024 * 1024
        ),
        name="gather_sum_exchange",
    )(wavenumber, spectral, legendre)

    block = 8
    flux = pl.pallas_call(
        functools.partial(synthesis_kernel, block),
        grid=(rows // block,),
        out_shape=jax.ShapeDtypeStruct((rows, NLONW, GROUP), BF16),
        in_specs=[
            pl.BlockSpec(memory_space=pltpu.VMEM),
            pl.BlockSpec(memory_space=pltpu.VMEM),
        ],
        out_specs=pl.BlockSpec((block, NLONW, GROUP), lambda i: (i, 0, 0)),
        compiler_params=pltpu.CompilerParams(vmem_limit_bytes=24 * 1024 * 1024),
        name="synthesis_product",
    )(table, rhs)
    return flux[None]


def solution(mesh):
    return jax.shard_map(
        functools.partial(shards, mesh.shape["wave"]),
        mesh=mesh,
        in_specs=(P(None, "wave", None, "lat", None), P("wave", None, None, "lat"), P()),
        out_specs=P("lat", "wave", None, None),
        check_vma=False,
    )
```

time: 96.8 us -> 84.1 us (0.87)
  Pallas kernels: 91.2 us -> 81.9 us
  local copies, waits for them, and re-layouts: 3.99 us -> 2.06 us
  other arithmetic: 1.38 us -> 0 us
    pallas_call x2, Pallas kernels: 91.2 us -> 81.9 us  [the longest x1 74.5 us: shards(): pl.pallas_call(functools.partial(exchange_kernel, waves), out_shape=[jax....]
    mul x6 -> x0, local copies, waits for them, and re-layouts: 1.19 us -> none  [the longest x2 0.84 us: fourier_table(): phase_index = wavenumber[None, :] * column[:, None] % period]
    unnamed x3 -> x4, local copies, waits for them, and re-layouts: 2.68 us -> 2.06 us
where the time goes in v2:
time: 84.1 us; the launch traced here: 84 us
  Pallas kernels  81.9 us (97%)
  local copies, waits for them, and re-layouts  2.06 us (2%)
    pallas_call x1, Pallas kernels, shards(): pl.pallas_call(functools.partial(exchange_kernel, waves), out_shape=[jax....  74.5 us
    pallas_call x1, Pallas kernels, shards(): pl.pallas_call(functools.partial(synthesis_kernel, block), grid=(rows //...  7.4 us
    unnamed x4, local copies, waits for them, and re-layouts  2.06 us

profile of v2, /device:TPU:1, one launch (start us, length us, event | category | flops | bytes accessed | tf_op | source)
XLA Modules:
  0.0 84.0 jit_solution(3809356850144170475)
XLA Ops:
  0.0 0.0 copy-start
  0.0 1.4 %copy-done = bf16[2,2,2,512,192]{3,4,2,1,0:T(8,128)(2,1)S(1)} copy-done((bf16[2,2,2,512,192]{3,4,2,1,0:T(8,128)(2,1)S(1)}, bf16[2,2,2,512,192]{3,4,2,1,0:T(8,128)(2,1)}, u32[]{:S(2)}) %copy-start) | copy-done | bytes 1572888
  1.4 0.0 copy-start.1
  1.4 0.7 copy-done.1
  2.1 74.5 %gather_sum_exchange.1 = (bf16[512,128]{1,0:T(8,128)(2,1)S(1)}, bf16[64,128,256]{2,1,0:T(8,128)(2,1)S(1)}) custom-call(s32[64]{0:T(128)S(1)} %copy-done.1, bf16[2,2,2,192,512]{4,3,2,1,0:T(8,128)(2,1)S(1)} %bitcast.2, bf16[2,2,2048,1024]{3,2,1,0:T(8,128)(2,1)} %leg_ref.1), custom_call_target="tpu_custom_call" | custom-call | tf_op jit(solution)/shard_map/gather_sum_exchange/pallas_call | solution.py:276
  76.6 7.4 %synthesis_product.1 = bf16[64,512,128]{2,1,0:T(8,128)(2,1)} custom-call(bf16[512,128]{1,0:T(8,128)(2,1)S(1)} %get-tuple-element.7.table_ref, bf16[64,128,256]{2,1,0:T(8,128)(2,1)S(1)} %get-tuple-element.8.rhs_ref), custom_call_target="tpu_custom_call" | custom-call | tf_op jit(solution)/shard_map/synthesis_product/pallas_call | solution.py:311
Async XLA Ops:
  0.0 1.4 %copy-start = (bf16[2,2,2,512,192]{3,4,2,1,0:T(8,128)(2,1)S(1)}, bf16[2,2,2,512,192]{3,4,2,1,0:T(8,128)(2,1)}, u32[]{:S(2)}) copy-start(bf16[2,2,2,512,192]{3,4,2,1,0:T(8,128)(2,1)} %param.3) | copy-start | bytes 4718596
  1.4 0.7 copy-start.1

commit v3 on v2

v3 whole, which is shorter than its diff:
```python
import functools
import math

import jax
import jax.numpy as jnp
from jax import lax
from jax.experimental import pallas as pl
from jax.experimental.pallas import tpu as pltpu
from jax.sharding import PartitionSpec as P

TRUNC = 7999
NLONW = 512
PERIOD = 2 * TRUNC + 2
MESH = pl.DeviceIdType.MESH
F32 = jnp.float32
BF16 = jnp.bfloat16
BANDS = 4
GROUP = 128


def exchange_kernel(
    waves, wn_hbm, spec_ref, leg_ref, table_ref, rhs_ref,
    xg, leg_v, sb, rv, wide, partial, wn_ref,
    wn_sem, leg_sem, own_sem, gs_sem, gr_sem, as_sem, ar_sem,
):
    wave = lax.axis_index("wave")
    lat = lax.axis_index("lat")
    plus, minus = lax.rem(lat + 1, BANDS), lax.rem(lat + BANDS - 1, BANDS)
    batches, slots, _, columns, depth = spec_ref.shape
    levels = columns // 6
    full = 3 * slots - 1
    rows = rv.shape[2]
    short = rows // 2
    narrow = GROUP // 2
    band = leg_ref.shape[3]
    tile = min(256, band)
    tiles = band // tile
    per = tile // rows
    half = waves // 2

    numbers = pltpu.make_async_copy(wn_hbm, wn_ref, wn_sem)
    numbers.start()

    def leg_copy(s):
        return pltpu.make_async_copy(leg_ref.at[s], leg_v.at[s], leg_sem.at[s])

    barrier = pltpu.get_barrier_semaphore()
    for other in (plus, minus):
        pl.semaphore_signal(barrier, inc=1, device_id=(wave, other), device_id_type=MESH)

    def greet(i, carry):
        peer = lax.rem(wave + i, waves)
        pl.semaphore_signal(barrier, inc=1, device_id=(peer, lat), device_id_type=MESH)
        return carry

    lax.fori_loop(1, waves, greet, 0)
    for s in range(slots):
        leg_copy(s).start()

    def prepare(s):
        first = wn_ref[wave * slots + s] + 2 * depth * lat
        slot_index = lax.broadcasted_iota(jnp.int32, (2 * levels, depth), 1)
        for p in range(2):
            live = first + p + 2 * slot_index <= TRUNC
            for b in range(batches):
                at = b * 2 * levels
                for r in range(2):
                    src = r * 3 * levels
                    vort = spec_ref[b, s, p, src : src + levels].astype(F32)
                    xg[s, 0, p, at + r * levels : at + (r + 1) * levels] = jnp.where(
                        live[:levels], vort, 0.0
                    ).astype(BF16)
                    wind = spec_ref[b, s, p, src + levels : src + 3 * levels].astype(F32)
                    xg[(1 + r) * slots + s, 0, p, at : at + 2 * levels] = jnp.where(live, wind, 0.0).astype(BF16)

    def gather_copy(g, i, part=None):
        src, dst, p, to = (
            (0, 3, 0, plus), (0, 3, 1, plus), (0, 1, 0, minus), (0, 1, 1, minus),
            (3, 2, 0, plus), (1, 2, 1, minus),
        )[i]
        piece = pl.ds(0, GROUP) if part is None else pl.ds(part * narrow, narrow)
        at = g if part is None else g + part
        return pltpu.make_async_remote_copy(
            src_ref=xg.at[g, src, p, piece],
            dst_ref=xg.at[g, dst, p, piece],
            send_sem=gs_sem.at[at, i],
            recv_sem=gr_sem.at[at, i],
            device_id=(wave, to),
            device_id_type=MESH,
        )

    def start_own(g, part=None):
        for i in (0, 3, 1, 2):
            gather_copy(g, i, part).start()

    def lines(part):
        return pl.ds(0, rows) if part is None else pl.ds(part * short, short)

    def self_copy(g, part=None):
        return pltpu.make_async_copy(
            sb.at[g, wave, lines(part)], rv.at[g, wave, lines(part)], own_sem.at[g + (part or 0)]
        )

    def all_of(g, part=None):
        peer = lax.rem(wave + 1, waves)
        return pltpu.make_async_remote_copy(
            src_ref=sb.at[g, pl.ds(0, waves - 1), lines(part)],
            dst_ref=rv.at[g, pl.ds(0, waves - 1), lines(part)],
            send_sem=as_sem.at[g + (part or 0)],
            recv_sem=ar_sem.at[g + (part or 0)],
            device_id=(peer, lat),
            device_id_type=MESH,
        )

    def make_table():
        lane = lax.broadcasted_iota(jnp.int32, (8, 2 * slots * waves), 1)
        slot = slots * lax.rem(lane, waves) + lax.rem(lane // waves, slots)
        number = jnp.zeros_like(lane)
        for n in range(slots * waves):
            number = jnp.where(slot == n, wn_ref[n], number)
        weight = jnp.where(number == 0, 1.0, 2.0).astype(F32)
        real = lane < slots * waves

        def block(i, carry):
            column = lax.broadcasted_iota(jnp.int32, lane.shape, 0)
            parts = []
            for n in range(2):
                product = number * (column + (16 * i + 8 * n))
                turns = jnp.floor(product.astype(F32) * (1.0 / PERIOD)).astype(jnp.int32)
                phase = product - turns * PERIOD
                phase = jnp.where(phase < 0, phase + PERIOD, phase)
                phase = jnp.where(phase >= PERIOD, phase - PERIOD, phase)
                angle = phase.astype(F32) * (2.0 * math.pi / PERIOD)
                parts.append(jnp.where(real, weight * jnp.cos(angle), -weight * jnp.sin(angle)))
            table_ref[pl.ds(pl.multiple_of(16 * i, 16), 16), :] = jnp.concatenate(parts, axis=0).astype(BF16)
            return carry

        lax.fori_loop(0, NLONW // 16, block, 0)

    def arrange(g):
        s = lax.rem(g, slots)
        t = g // slots
        all_of(g).wait_recv()
        self_copy(g).wait()
        wide[...] = rv[g].astype(F32).reshape(waves * rows, GROUP)

        @pl.when(t == 0)
        def _():
            lane = lax.broadcasted_iota(jnp.int32, (waves, GROUP), 1)
            real_lane = lax.rem(lane // levels, 2) == 0

            def latitude(q, carry):
                x = wide[pl.ds(q, waves, stride=rows), :]
                real = jnp.where(real_lane, x, pltpu.roll(x, levels, 1))
                imag = jnp.where(real_lane, pltpu.roll(x, GROUP - levels, 1), x)
                rhs_ref[q, pl.ds(s * waves, waves), 0:GROUP] = real.astype(BF16)
                rhs_ref[q, pl.ds((slots + s) * waves, waves), 0:GROUP] = imag.astype(BF16)
                return carry

            lax.fori_loop(0, rows, latitude, 0, unroll=8)

        @pl.when(t > 0)
        def _():
            def latitude(q, carry):
                x = wide[pl.ds(q, waves, stride=rows), :]
                rhs_ref[q, pl.ds((g - slots) * waves, waves), GROUP : 2 * GROUP] = x.astype(BF16)
                return carry

            lax.fori_loop(0, rows, latitude, 0, unroll=8)

    def arrange_half(part):
        all_of(full, part).wait_recv()
        self_copy(full, part).wait()
        wide[0 : waves * short] = rv[full, :, part * short : (part + 1) * short].astype(F32).reshape(
            waves * short, GROUP
        )
        at = pl.ds((full - slots) * waves, waves)

        def latitude(q, carry):
            x = wide[pl.ds(q, waves, stride=short), :]
            turned = pltpu.roll(x, narrow, 1)
            first, second = (x, turned) if part == 0 else (turned, x)
            cut = slice(part * narrow, (part + 1) * narrow)
            into = slice(GROUP + part * narrow, GROUP + (part + 1) * narrow)
            rhs_ref[q, at, into] = first[:, cut].astype(BF16)
            rhs_ref[q + short, at, into] = second[:, cut].astype(BF16)
            return carry

        lax.fori_loop(0, short, latitude, 0, unroll=8)

    def product(g, s, part, n, sources):
        piece = slice(0, GROUP) if part is None else slice(part * narrow, (part + 1) * narrow)
        total = []
        for p in range(2):
            acc = None
            for j in sources:
                k0 = pl.multiple_of(lax.rem(lat + j, BANDS) * depth, depth)
                poly = leg_v[s, p, pl.ds(k0, depth), pl.ds(pl.multiple_of(n * tile, tile), tile)]
                add = jnp.dot(xg[g, j, p, piece], poly, preferred_element_type=F32)
                acc = add if acc is None else acc + add
            total.append(acc)
        return total

    def begin(g, s, part):
        for i in (1, 2):
            gather_copy(g, i, part).wait_recv()

        def columns_tile(n, inner):
            partial[n, 0], partial[n, 1] = product(g, s, part, n, (0, 1, 3))
            return inner

        lax.fori_loop(0, tiles, columns_tile, 0)
        for i in (4, 5):
            gather_copy(g, i, part).wait_recv()

    def multiply(g, s, part=None):
        def columns_tile(turn, inner):
            n = lax.rem(turn + wave, tiles)
            if part is None:
                total = product(g, s, part, n, (0, 1, 3, 2))
            else:
                total = product(g, s, part, n, (2,))
                total = [total[p] + partial[n, p] for p in range(2)]
            for at, value in ((0, total[0] + total[1]), (half, total[0] - total[1])):
                if part is None:
                    sb[g, pl.ds(at + n * per, per)] = value.T.astype(BF16).reshape(per, rows, GROUP)
                else:
                    turned = value.T.reshape(per, rows, narrow)
                    packed = jnp.concatenate([turned[:, :short], turned[:, short:]], axis=2)
                    sb[g, pl.ds(at + n * per, per), part * short : (part + 1) * short] = packed.astype(BF16)

            def send(i, after):
                peer = n * per + lax.rem(i, per) + half * (i // per)

                @pl.when(peer != wave)
                def _():
                    pltpu.make_async_remote_copy(
                        src_ref=sb.at[g, peer, lines(part)],
                        dst_ref=rv.at[g, wave, lines(part)],
                        send_sem=as_sem.at[g + (part or 0)],
                        recv_sem=ar_sem.at[g + (part or 0)],
                        device_id=(peer, lat),
                        device_id_type=MESH,
                    ).start()

                return after

            lax.fori_loop(0, 2 * per, send, 0)
            return inner

        lax.fori_loop(0, tiles, columns_tile, 0)
        self_copy(g, part).start()

    def hand_on(g, part=None):
        gather_copy(g, 0, part).wait_recv()
        gather_copy(g, 4, part).start()
        gather_copy(g, 3, part).wait_recv()
        gather_copy(g, 5, part).start()

    def rest(g, part=None):
        for i in (1, 2, 4, 5):
            gather_copy(g, i, part).wait_recv()

    numbers.wait()
    prepare(0)
    pl.semaphore_wait(barrier, waves + 1)
    start_own(0)
    for s in range(1, slots):
        prepare(s)
    make_table()
    hand_on(0)
    start_own(1)

    def step(g, carry):
        @pl.when(g + 1 < full)
        def _():
            hand_on(g + 1)

        @pl.when(g + 2 < full)
        def _():
            start_own(g + 2)

        @pl.when(g + 2 == full)
        def _():
            start_own(full, 0)

        @pl.when(g + 1 == full)
        def _():
            hand_on(full, 0)
            start_own(full, 1)

        rest(g)

        @pl.when(g < slots)
        def _():
            leg_copy(g).wait()

        multiply(g, lax.rem(g, slots))

        @pl.when((g >= 2) & (g < full - 1))
        def _():
            arrange(g - 2)

        return carry

    lax.fori_loop(0, full, step, 0)
    begin(full, slots - 1, 0)
    hand_on(full, 1)
    multiply(full, slots - 1, 0)
    begin(full, slots - 1, 1)
    multiply(full, slots - 1, 1)
    for g in (full - 3, full - 2, full - 1):
        arrange(g)
    for part in range(2):
        arrange_half(part)

    def finish(g, carry):
        for i in range(6):
            gather_copy(g, i).wait_send()
        all_of(g).wait_send()
        return carry

    lax.fori_loop(0, full, finish, 0)
    for part in range(2):
        for i in range(6):
            gather_copy(full, i, part).wait_send()
        all_of(full, part).wait_send()


def synthesis_kernel(block, table_ref, rhs_ref, out_ref, made, out_sem):
    rows = rhs_ref.shape[0]

    def out_copy(i):
        piece = pl.ds(i * 8, 8)
        return pltpu.make_async_copy(made.at[piece], out_ref.at[piece], out_sem.at[i])

    def step(i, carry):
        for n in range(block):
            q = i * block + n
            grid = jnp.dot(table_ref[...], rhs_ref[q], preferred_element_type=F32)
            made[q] = (grid[:, :GROUP] * grid[:, GROUP:]).astype(BF16)
            if n % 8 == 8-1:
                out_copy(n // 8).start()
        return carry

    lax.fori_loop(0, rows // block, step, 0)

    def finish(i, carry):
        out_copy(i).wait()
        return carry

    lax.fori_loop(0, rows // 8, finish, 0)


def shards(waves, spectral, legendre, wavenumber):
    spectral = jnp.swapaxes(spectral, 3, 4)
    slots = spectral.shape[1]
    depth = spectral.shape[4]
    rows = 2 * legendre.shape[3] // waves
    band = legendre.shape[3]
    tiles = max(1, band // 256)
    chunks = 3 * slots
    inner = 2 * slots * waves

    table, rhs = pl.pallas_call(
        functools.partial(exchange_kernel, waves),
        out_shape=[
            jax.ShapeDtypeStruct((NLONW, inner), BF16),
            jax.ShapeDtypeStruct((rows, inner, 2 * GROUP), BF16),
        ],
        in_specs=[
            pl.BlockSpec(memory_space=pl.ANY),
            pl.BlockSpec(memory_space=pltpu.VMEM),
            pl.BlockSpec(memory_space=pl.ANY),
        ],
        out_specs=[pl.BlockSpec(memory_space=pltpu.VMEM)] * 2,
        scratch_shapes=[
            pltpu.VMEM((chunks, BANDS, 2, GROUP, depth), BF16),
            pltpu.VMEM(legendre.shape, BF16),
            pltpu.VMEM((chunks, waves, rows, GROUP), BF16),
            pltpu.VMEM((chunks, waves, rows, GROUP), BF16),
            pltpu.VMEM((waves * rows, GROUP), F32),
            pltpu.VMEM((tiles, 2, GROUP // 2, band // tiles), F32),
            pltpu.SMEM((slots * waves,), jnp.int32),
            pltpu.SemaphoreType.DMA,
            pltpu.SemaphoreType.DMA((slots,)),
            pltpu.SemaphoreType.DMA((chunks + 1,)),
            pltpu.SemaphoreType.DMA((chunks + 1, 6)),
            pltpu.SemaphoreType.DMA((chunks + 1, 6)),
            pltpu.SemaphoreType.DMA((chunks + 1,)),
            pltpu.SemaphoreType.DMA((chunks + 1,)),
        ],
        compiler_params=pltpu.CompilerParams(
            collective_id=0, has_side_effects=True, vmem_limit_bytes=36 * 1024 * 1024
        ),
        name="gather_sum_exchange",
    )(wavenumber, spectral, legendre)

    block = 64
    flux = pl.pallas_call(
        functools.partial(synthesis_kernel, block),
        out_shape=jax.ShapeDtypeStruct((rows, NLONW, GROUP), BF16),
        in_specs=[pl.BlockSpec(memory_space=pltpu.VMEM)] * 2,
        out_specs=pl.BlockSpec(memory_space=pl.ANY),
        scratch_shapes=[
            pltpu.VMEM((rows, NLONW, GROUP), BF16),
            pltpu.SemaphoreType.DMA((rows // 8,)),
        ],
        compiler_params=pltpu.CompilerParams(vmem_limit_bytes=24 * 1024 * 1024),
        name="synthesis_product",
    )(table, rhs)
    return flux[None]


def solution(mesh):
    return jax.shard_map(
        functools.partial(shards, mesh.shape["wave"]),
        mesh=mesh,
        in_specs=(P(None, "wave", None, "lat", None), P("wave", None, None, "lat"), P()),
        out_specs=P("lat", "wave", None, None),
        check_vma=False,
    )
```

time: 84.1 us -> 79.7 us (0.948)
  Pallas kernels: 81.9 us -> 77.5 us
    pallas_call x1, Pallas kernels: 74.5 us -> 71.9 us  [shards(): pl.pallas_call(functools.partial(exchange_kernel, waves), out_shape=[jax....]
    pallas_call x1, Pallas kernels: 7.4 us -> 5.56 us  [shards(): pl.pallas_call(functools.partial(synthesis_kernel, block), out_shape=jax....]
where the time goes in v3:
time: 79.7 us; the launch traced here: 79.6 us
  Pallas kernels  77.5 us (97%)
  local copies, waits for them, and re-layouts  2.06 us (3%)
    pallas_call x1, Pallas kernels, shards(): pl.pallas_call(functools.partial(exchange_kernel, waves), out_shape=[jax....  71.9 us
    pallas_call x1, Pallas kernels, shards(): pl.pallas_call(functools.partial(synthesis_kernel, block), out_shape=jax....  5.56 us
    unnamed x4, local copies, waits for them, and re-layouts  2.06 us

profile of v3, /device:TPU:1, one launch (start us, length us, event | category | flops | bytes accessed | tf_op | source)
XLA Modules:
  0.0 79.6 jit_solution(93671998004057843)
XLA Ops:
  0.0 0.0 copy-start
  0.0 1.4 %copy-done = bf16[2,2,2,512,192]{3,4,2,1,0:T(8,128)(2,1)S(1)} copy-done((bf16[2,2,2,512,192]{3,4,2,1,0:T(8,128)(2,1)S(1)}, bf16[2,2,2,512,192]{3,4,2,1,0:T(8,128)(2,1)}, u32[]{:S(2)}) %copy-start) | copy-done | bytes 1572888
  1.4 0.0 copy-start.1
  1.4 0.7 copy-done.1
  2.1 71.9 %gather_sum_exchange.1 = (bf16[512,128]{1,0:T(8,128)(2,1)S(1)}, bf16[64,128,256]{2,1,0:T(8,128)(2,1)S(1)}) custom-call(s32[64]{0:T(128)S(1)} %copy-done.1, bf16[2,2,2,192,512]{4,3,2,1,0:T(8,128)(2,1)S(1)} %bitcast.2, bf16[2,2,2048,1024]{3,2,1,0:T(8,128)(2,1)} %leg_ref.1), custom_call_target="tpu_custom_call" | custom-call | tf_op jit(solution)/shard_map/gather_sum_exchange/pallas_call | solution.py:365
  74.0 5.6 %synthesis_product.1 = bf16[64,512,128]{2,1,0:T(8,128)(2,1)} custom-call(bf16[512,128]{1,0:T(8,128)(2,1)S(1)} %get-tuple-element.7.table_ref, bf16[64,128,256]{2,1,0:T(8,128)(2,1)S(1)} %get-tuple-element.8.rhs_ref), custom_call_target="tpu_custom_call" | custom-call | tf_op jit(solution)/shard_map/synthesis_product/pallas_call | solution.py:400
Async XLA Ops:
  0.0 1.4 %copy-start = (bf16[2,2,2,512,192]{3,4,2,1,0:T(8,128)(2,1)S(1)}, bf16[2,2,2,512,192]{3,4,2,1,0:T(8,128)(2,1)}, u32[]{:S(2)}) copy-start(bf16[2,2,2,512,192]{3,4,2,1,0:T(8,128)(2,1)} %param.3) | copy-start | bytes 4718596
  1.4 0.7 copy-start.1

commit v4 on v3

--- a/solution.py
+++ b/solution.py
@@ -19,8 +19,8 @@
 
 
 def exchange_kernel(
-    waves, wn_hbm, spec_ref, leg_ref, table_ref, rhs_ref,
-    xg, leg_v, sb, rv, wide, partial, wn_ref,
+    waves, wn_hbm, spec_ref, leg_ref, table_ref, wind_ref, vort_ref,
+    xg, leg_v, sb, rv, wide, early, early_last, held, wn_ref,
     wn_sem, leg_sem, own_sem, gs_sem, gr_sem, as_sem, ar_sem,
 ):
     wave = lax.axis_index("wave")
@@ -153,8 +153,8 @@
                 x = wide[pl.ds(q, waves, stride=rows), :]
                 real = jnp.where(real_lane, x, pltpu.roll(x, levels, 1))
                 imag = jnp.where(real_lane, pltpu.roll(x, GROUP - levels, 1), x)
-                rhs_ref[q, pl.ds(s * waves, waves), 0:GROUP] = real.astype(BF16)
-                rhs_ref[q, pl.ds((slots + s) * waves, waves), 0:GROUP] = imag.astype(BF16)
+                held[q, pl.ds(s * waves, waves), :] = real.astype(BF16)
+                held[q, pl.ds((slots + s) * waves, waves), :] = imag.astype(BF16)
                 return carry
 
             lax.fori_loop(0, rows, latitude, 0, unroll=8)
@@ -163,7 +163,7 @@
         def _():
             def latitude(q, carry):
                 x = wide[pl.ds(q, waves, stride=rows), :]
-                rhs_ref[q, pl.ds((g - slots) * waves, waves), GROUP : 2 * GROUP] = x.astype(BF16)
+                wind_ref[q, pl.ds((g - slots) * waves, waves), :] = x.astype(BF16)
                 return carry
 
             lax.fori_loop(0, rows, latitude, 0, unroll=8)
@@ -181,9 +181,8 @@
             turned = pltpu.roll(x, narrow, 1)
             first, second = (x, turned) if part == 0 else (turned, x)
             cut = slice(part * narrow, (part + 1) * narrow)
-            into = slice(GROUP + part * narrow, GROUP + (part + 1) * narrow)
-            rhs_ref[q, at, into] = first[:, cut].astype(BF16)
-            rhs_ref[q + short, at, into] = second[:, cut].astype(BF16)
+            wind_ref[q, at, cut] = first[:, cut].astype(BF16)
+            wind_ref[q + short, at, cut] = second[:, cut].astype(BF16)
             return carry
 
         lax.fori_loop(0, short, latitude, 0, unroll=8)
@@ -201,26 +200,53 @@
             total.append(acc)
         return total
 
-    def begin(g, s, part):
+    def synthesize_vorticity(first, count):
+        def pairs(i, carry):
+            for n in range(4):
+                q = first + 8 * i + 2 * n
+                rhs = jnp.concatenate([held[q], held[q + 1]], axis=1)
+                grid = jnp.dot(table_ref[...], rhs, preferred_element_type=F32)
+                vort_ref[q] = grid[:, :GROUP].astype(BF16)
+                vort_ref[q + 1] = grid[:, GROUP:].astype(BF16)
+            return carry
+
+        lax.fori_loop(0, count // 8, pairs, 0)
+
+    def begin_last():
+        def columns_tile(n, inner):
+            early_last[n, 0], early_last[n, 1] = product(full, slots - 1, None, n, (0,))
+            return inner
+
+        lax.fori_loop(0, tiles, columns_tile, 0)
+
+    def begin(g, s, part=None):
         for i in (1, 2):
             gather_copy(g, i, part).wait_recv()
 
         def columns_tile(n, inner):
-            partial[n, 0], partial[n, 1] = product(g, s, part, n, (0, 1, 3))
+            if part is None:
+                early[n, 0], early[n, 1] = product(g, s, part, n, (0, 1, 3))
+            else:
+                piece = slice(part * narrow, (part + 1) * narrow)
+                more = product(g, s, part, n, (1, 3))
+                for p in range(2):
+                    early_last[n, p, piece] += more[p]
             return inner
 
         lax.fori_loop(0, tiles, columns_tile, 0)
+
+    def multiply(g, s, part=None):
         for i in (4, 5):
             gather_copy(g, i, part).wait_recv()
 
-    def multiply(g, s, part=None):
         def columns_tile(turn, inner):
             n = lax.rem(turn + wave, tiles)
+            total = product(g, s, part, n, (2,))
             if part is None:
-                total = product(g, s, part, n, (0, 1, 3, 2))
+                total = [total[p] + early[n, p] for p in range(2)]
             else:
-                total = product(g, s, part, n, (2,))
-                total = [total[p] + partial[n, p] for p in range(2)]
+                piece = slice(part * narrow, (part + 1) * narrow)
+                total = [total[p] + early_last[n, p, piece] for p in range(2)]
             for at, value in ((0, total[0] + total[1]), (half, total[0] - total[1])):
                 if part is None:
                     sb[g, pl.ds(at + n * per, per)] = value.T.astype(BF16).reshape(per, rows, GROUP)
@@ -257,10 +283,6 @@
         gather_copy(g, 3, part).wait_recv()
         gather_copy(g, 5, part).start()
 
-    def rest(g, part=None):
-        for i in (1, 2, 4, 5):
-            gather_copy(g, i, part).wait_recv()
-
     numbers.wait()
     prepare(0)
     pl.semaphore_wait(barrier, waves + 1)
@@ -270,6 +292,8 @@
     make_table()
     hand_on(0)
     start_own(1)
+    leg_copy(0).wait()
+    begin(0, 0)
 
     def step(g, carry):
         @pl.when(g + 1 < full)
@@ -289,17 +313,31 @@
             hand_on(full, 0)
             start_own(full, 1)
 
-        rest(g)
-
-        @pl.when(g < slots)
-        def _():
-            leg_copy(g).wait()
-
         multiply(g, lax.rem(g, slots))
 
-        @pl.when((g >= 2) & (g < full - 1))
-        def _():
-            arrange(g - 2)
+        @pl.when(g == slots + 1)
+        def _():
+            synthesize_vorticity(rows // 2, rows // 2)
+
+        @pl.when(g + 1 < slots)
+        def _():
+            leg_copy(g + 1).wait()
+
+        @pl.when(g + 1 < full)
+        def _():
+            begin(g + 1, lax.rem(g + 1, slots))
+
+        @pl.when(g + 2 == full)
+        def _():
+            begin_last()
+
+        @pl.when((g >= 1) & (g < full - 1))
+        def _():
+            arrange(g - 1)
+
+        @pl.when(g == slots)
+        def _():
+            synthesize_vorticity(0, rows // 2)
 
         return carry
 
@@ -309,7 +347,7 @@
     multiply(full, slots - 1, 0)
     begin(full, slots - 1, 1)
     multiply(full, slots - 1, 1)
-    for g in (full - 3, full - 2, full - 1):
+    for g in (full - 2, full - 1):
         arrange(g)
     for part in range(2):
         arrange_half(part)
@@ -327,29 +365,26 @@
         all_of(full, part).wait_send()
 
 
-def synthesis_kernel(block, table_ref, rhs_ref, out_ref, made, out_sem):
-    rows = rhs_ref.shape[0]
+def synthesis_kernel(block, table_ref, wind_ref, vort_ref, out_ref, made, out_sem):
+    rows = wind_ref.shape[0]
 
     def out_copy(i):
-        piece = pl.ds(i * 8, 8)
+        piece = pl.ds(i * block, block)
         return pltpu.make_async_copy(made.at[piece], out_ref.at[piece], out_sem.at[i])
 
-    def step(i, carry):
-        for n in range(block):
-            q = i * block + n
-            grid = jnp.dot(table_ref[...], rhs_ref[q], preferred_element_type=F32)
-            made[q] = (grid[:, :GROUP] * grid[:, GROUP:]).astype(BF16)
-            if n % 8 == 8-1:
-                out_copy(n // 8).start()
-        return carry
-
-    lax.fori_loop(0, rows // block, step, 0)
+    for q in range(0, rows, 2):
+        rhs = jnp.concatenate([wind_ref[q], wind_ref[q + 1]], axis=1)
+        grid = jnp.dot(table_ref[...], rhs, preferred_element_type=F32)
+        made[q] = (vort_ref[q].astype(F32) * grid[:, :GROUP]).astype(BF16)
+        made[q + 1] = (vort_ref[q + 1].astype(F32) * grid[:, GROUP:]).astype(BF16)
+        if (q + 2) % block == 0:
+            out_copy(q // block).start()
 
     def finish(i, carry):
         out_copy(i).wait()
         return carry
 
-    lax.fori_loop(0, rows // 8, finish, 0)
+    lax.fori_loop(0, rows // block, finish, 0)
 
 
 def shards(waves, spectral, legendre, wavenumber):
@@ -362,25 +397,28 @@
     chunks = 3 * slots
     inner = 2 * slots * waves
 
-    table, rhs = pl.pallas_call(
+    table, wind, vort = pl.pallas_call(
         functools.partial(exchange_kernel, waves),
         out_shape=[
             jax.ShapeDtypeStruct((NLONW, inner), BF16),
-            jax.ShapeDtypeStruct((rows, inner, 2 * GROUP), BF16),
+            jax.ShapeDtypeStruct((rows, inner, GROUP), BF16),
+            jax.ShapeDtypeStruct((rows, NLONW, GROUP), BF16),
         ],
         in_specs=[
             pl.BlockSpec(memory_space=pl.ANY),
             pl.BlockSpec(memory_space=pltpu.VMEM),
             pl.BlockSpec(memory_space=pl.ANY),
         ],
-        out_specs=[pl.BlockSpec(memory_space=pltpu.VMEM)] * 2,
+        out_specs=[pl.BlockSpec(memory_space=pltpu.VMEM)] * 3,
         scratch_shapes=[
             pltpu.VMEM((chunks, BANDS, 2, GROUP, depth), BF16),
             pltpu.VMEM(legendre.shape, BF16),
             pltpu.VMEM((chunks, waves, rows, GROUP), BF16),
             pltpu.VMEM((chunks, waves, rows, GROUP), BF16),
             pltpu.VMEM((waves * rows, GROUP), F32),
-            pltpu.VMEM((tiles, 2, GROUP // 2, band // tiles), F32),
+            pltpu.VMEM((tiles, 2, GROUP, band // tiles), F32),
+            pltpu.VMEM((tiles, 2, GROUP, band // tiles), F32),
+            pltpu.VMEM((rows, inner, GROUP), BF16),
             pltpu.SMEM((slots * waves,), jnp.int32),
             pltpu.SemaphoreType.DMA,
             pltpu.SemaphoreType.DMA((slots,)),
@@ -391,24 +429,24 @@
             pltpu.SemaphoreType.DMA((chunks + 1,)),
         ],
         compiler_params=pltpu.CompilerParams(
-            collective_id=0, has_side_effects=True, vmem_limit_bytes=36 * 1024 * 1024
+            collective_id=0, has_side_effects=True, vmem_limit_bytes=38 * 1024 * 1024
         ),
         name="gather_sum_exchange",
     )(wavenumber, spectral, legendre)
 
-    block = 64
+    block = 8
     flux = pl.pallas_call(
         functools.partial(synthesis_kernel, block),
         out_shape=jax.ShapeDtypeStruct((rows, NLONW, GROUP), BF16),
-        in_specs=[pl.BlockSpec(memory_space=pltpu.VMEM)] * 2,
+        in_specs=[pl.BlockSpec(memory_space=pltpu.VMEM)] * 3,
         out_specs=pl.BlockSpec(memory_space=pl.ANY),
         scratch_shapes=[
             pltpu.VMEM((rows, NLONW, GROUP), BF16),
-            pltpu.SemaphoreType.DMA((rows // 8,)),
+            pltpu.SemaphoreType.DMA((rows // block,)),
         ],
         compiler_params=pltpu.CompilerParams(vmem_limit_bytes=24 * 1024 * 1024),
         name="synthesis_product",
-    )(table, rhs)
+    )(table, wind, vort)
     return flux[None]
 
 

time: 79.7 us -> 78.2 us (0.981)
  Pallas kernels: 77.5 us -> 76 us
    pallas_call x1, Pallas kernels: 5.56 us -> 3.79 us  [shards(): pl.pallas_call(functools.partial(synthesis_kernel, block), out_shape=jax....]
where the time goes in v4:
time: 78.2 us; the launch traced here: 78 us
  Pallas kernels  76 us (97%)
  local copies, waits for them, and re-layouts  2.06 us (3%)
    pallas_call x1, Pallas kernels, shards(): pl.pallas_call(functools.partial(exchange_kernel, waves), out_shape=[jax....  72.2 us
    pallas_call x1, Pallas kernels, shards(): pl.pallas_call(functools.partial(synthesis_kernel, block), out_shape=jax....  3.79 us
    unnamed x4, local copies, waits for them, and re-layouts  2.06 us

profile of v4, /device:TPU:1, one launch (start us, length us, event | category | flops | bytes accessed | tf_op | source)
XLA Modules:
  0.0 78.0 jit_solution(13218997451055870054)
XLA Ops:
  0.0 0.0 copy-start
  0.0 1.4 %copy-done = bf16[2,2,2,512,192]{3,4,2,1,0:T(8,128)(2,1)S(1)} copy-done((bf16[2,2,2,512,192]{3,4,2,1,0:T(8,128)(2,1)S(1)}, bf16[2,2,2,512,192]{3,4,2,1,0:T(8,128)(2,1)}, u32[]{:S(2)}) %copy-start) | copy-done | bytes 1572888
  1.4 0.0 copy-start.1
  1.4 0.7 copy-done.1
  2.1 72.2 %gather_sum_exchange.1 = (bf16[512,128]{1,0:T(8,128)(2,1)S(1)}, bf16[64,128,128]{2,1,0:T(8,128)(2,1)S(1)}, bf16[64,512,128]{2,1,0:T(8,128)(2,1)S(1)}) custom-call(s32[64]{0:T(128)S(1)} %copy-done.1, bf16[2,2,2,192,512]{4,3,2,1,0:T(8,128)(2,1)S(1)} %bitcast.2, bf16[2,2,2048,1024]{3,2,1,0:T(8,128)(2,1)} %leg_ref.1), custom_call_target="tpu_custom_call" | custom-call | tf_op jit(solution)/shard_map/gather_sum_exchange/pallas_call | solution.py:400
  74.3 3.8 %synthesis_product.1 = bf16[64,512,128]{2,1,0:T(8,128)(2,1)} custom-call(bf16[512,128]{1,0:T(8,128)(2,1)S(1)} %get-tuple-element.8.table_ref, bf16[64,128,128]{2,1,0:T(8,128)(2,1)S(1)} %get-tuple-element.9.wind_ref, bf16[64,512,128]{2,1,0:T(8,128)(2,1)S(1)} %get-tuple-element.10.vort_ref), custom_call_target="tpu_custom_call" | custom-call | tf_op jit(solution)/shard_map/synthesis_product/pallas_call | solution.py:438
Async XLA Ops:
  0.0 1.4 %copy-start = (bf16[2,2,2,512,192]{3,4,2,1,0:T(8,128)(2,1)S(1)}, bf16[2,2,2,512,192]{3,4,2,1,0:T(8,128)(2,1)}, u32[]{:S(2)}) copy-start(bf16[2,2,2,512,192]{3,4,2,1,0:T(8,128)(2,1)} %param.3) | copy-start | bytes 4718596
  1.4 0.7 copy-start.1

commit v5 on v4

--- a/solution.py
+++ b/solution.py
@@ -33,7 +33,7 @@
     short = rows // 2
     narrow = GROUP // 2
     band = leg_ref.shape[3]
-    tile = min(256, band)
+    tile = min(512, band)
     tiles = band // tile
     per = tile // rows
     half = waves // 2
@@ -393,7 +393,7 @@
     depth = spectral.shape[4]
     rows = 2 * legendre.shape[3] // waves
     band = legendre.shape[3]
-    tiles = max(1, band // 256)
+    tiles = max(1, band // 512)
     chunks = 3 * slots
     inner = 2 * slots * waves
 

time: 78.2 us -> 77.6 us (level)
  no operation moved by 1% of the time
where the time goes in v5:
time: 77.6 us; the launch traced here: 77.5 us
  Pallas kernels  75.4 us (97%)
  local copies, waits for them, and re-layouts  2.06 us (3%)
    pallas_call x1, Pallas kernels, shards(): pl.pallas_call(functools.partial(exchange_kernel, waves), out_shape=[jax....  71.6 us
    pallas_call x1, Pallas kernels, shards(): pl.pallas_call(functools.partial(synthesis_kernel, block), out_shape=jax....  3.79 us
    unnamed x4, local copies, waits for them, and re-layouts  2.06 us

profile of v5, /device:TPU:1, one launch (start us, length us, event | category | flops | bytes accessed | tf_op | source)
XLA Modules:
  0.0 77.5 jit_solution(7750783633642257423)
XLA Ops:
  0.0 0.0 copy-start
  0.0 1.4 %copy-done = bf16[2,2,2,512,192]{3,4,2,1,0:T(8,128)(2,1)S(1)} copy-done((bf16[2,2,2,512,192]{3,4,2,1,0:T(8,128)(2,1)S(1)}, bf16[2,2,2,512,192]{3,4,2,1,0:T(8,128)(2,1)}, u32[]{:S(2)}) %copy-start) | copy-done | bytes 1572888
  1.4 0.0 copy-start.1
  1.4 0.7 copy-done.1
  2.1 71.6 %gather_sum_exchange.1 = (bf16[512,128]{1,0:T(8,128)(2,1)S(1)}, bf16[64,128,128]{2,1,0:T(8,128)(2,1)S(1)}, bf16[64,512,128]{2,1,0:T(8,128)(2,1)S(1)}) custom-call(s32[64]{0:T(128)S(1)} %copy-done.1, bf16[2,2,2,192,512]{4,3,2,1,0:T(8,128)(2,1)S(1)} %bitcast.2, bf16[2,2,2048,1024]{3,2,1,0:T(8,128)(2,1)} %leg_ref.1), custom_call_target="tpu_custom_call" | custom-call | tf_op jit(solution)/shard_map/gather_sum_exchange/pallas_call | solution.py:400
  73.7 3.8 %synthesis_product.1 = bf16[64,512,128]{2,1,0:T(8,128)(2,1)} custom-call(bf16[512,128]{1,0:T(8,128)(2,1)S(1)} %get-tuple-element.8.table_ref, bf16[64,128,128]{2,1,0:T(8,128)(2,1)S(1)} %get-tuple-element.9.wind_ref, bf16[64,512,128]{2,1,0:T(8,128)(2,1)S(1)} %get-tuple-element.10.vort_ref), custom_call_target="tpu_custom_call" | custom-call | tf_op jit(solution)/shard_map/synthesis_product/pallas_call | solution.py:438
Async XLA Ops:
  0.0 1.4 %copy-start = (bf16[2,2,2,512,192]{3,4,2,1,0:T(8,128)(2,1)S(1)}, bf16[2,2,2,512,192]{3,4,2,1,0:T(8,128)(2,1)}, u32[]{:S(2)}) copy-start(bf16[2,2,2,512,192]{3,4,2,1,0:T(8,128)(2,1)} %param.3) | copy-start | bytes 4718596
  1.4 0.7 copy-start.1

commit v6 on v5

--- a/solution.py
+++ b/solution.py
@@ -57,7 +57,7 @@
     for s in range(slots):
         leg_copy(s).start()
 
-    def prepare(s):
+    def prepare(s, winds):
         first = wn_ref[wave * slots + s] + 2 * depth * lat
         slot_index = lax.broadcasted_iota(jnp.int32, (2 * levels, depth), 1)
         for p in range(2):
@@ -66,12 +66,14 @@
                 at = b * 2 * levels
                 for r in range(2):
                     src = r * 3 * levels
-                    vort = spec_ref[b, s, p, src : src + levels].astype(F32)
-                    xg[s, 0, p, at + r * levels : at + (r + 1) * levels] = jnp.where(
-                        live[:levels], vort, 0.0
-                    ).astype(BF16)
-                    wind = spec_ref[b, s, p, src + levels : src + 3 * levels].astype(F32)
-                    xg[(1 + r) * slots + s, 0, p, at : at + 2 * levels] = jnp.where(live, wind, 0.0).astype(BF16)
+                    if winds:
+                        wind = spec_ref[b, s, p, src + levels : src + 3 * levels].astype(F32)
+                        xg[(1 + r) * slots + s, 0, p, at : at + 2 * levels] = jnp.where(live, wind, 0.0).astype(BF16)
+                    else:
+                        vort = spec_ref[b, s, p, src : src + levels].astype(F32)
+                        xg[s, 0, p, at + r * levels : at + (r + 1) * levels] = jnp.where(
+                            live[:levels], vort, 0.0
+                        ).astype(BF16)
 
     def gather_copy(g, i, part=None):
         src, dst, p, to = (
@@ -284,11 +286,13 @@
         gather_copy(g, 5, part).start()
 
     numbers.wait()
-    prepare(0)
+    prepare(0, False)
     pl.semaphore_wait(barrier, waves + 1)
     start_own(0)
     for s in range(1, slots):
-        prepare(s)
+        prepare(s, False)
+    for s in range(slots):
+        prepare(s, True)
     make_table()
     hand_on(0)
     start_own(1)
@@ -349,8 +353,6 @@
     multiply(full, slots - 1, 1)
     for g in (full - 2, full - 1):
         arrange(g)
-    for part in range(2):
-        arrange_half(part)
 
     def finish(g, carry):
         for i in range(6):
@@ -362,7 +364,10 @@
     for part in range(2):
         for i in range(6):
             gather_copy(full, i, part).wait_send()
-        all_of(full, part).wait_send()
+    all_of(full, 0).wait_send()
+    for part in range(2):
+        arrange_half(part)
+    all_of(full, 1).wait_send()
 
 
 def synthesis_kernel(block, table_ref, wind_ref, vort_ref, out_ref, made, out_sem):
@@ -434,7 +439,7 @@
         name="gather_sum_exchange",
     )(wavenumber, spectral, legendre)
 
-    block = 8
+    block = 4
     flux = pl.pallas_call(
         functools.partial(synthesis_kernel, block),
         out_shape=jax.ShapeDtypeStruct((rows, NLONW, GROUP), BF16),

time: 77.6 us -> 77.5 us (level)
  no operation moved by 1% of the time
where the time goes in v6:
time: 77.5 us; the launch traced here: 77.3 us
  Pallas kernels  75.2 us (97%)
  local copies, waits for them, and re-layouts  2.06 us (3%)
    pallas_call x1, Pallas kernels, shards(): pl.pallas_call(functools.partial(exchange_kernel, waves), out_shape=[jax....  71.5 us
    pallas_call x1, Pallas kernels, shards(): pl.pallas_call(functools.partial(synthesis_kernel, block), out_shape=jax....  3.7 us
    unnamed x4, local copies, waits for them, and re-layouts  2.06 us

profile of v6, /device:TPU:1, one launch (start us, length us, event | category | flops | bytes accessed | tf_op | source)
XLA Modules:
  0.0 77.3 jit_solution(6482464509760485432)
XLA Ops:
  0.0 0.0 copy-start
  0.0 1.4 %copy-done = bf16[2,2,2,512,192]{3,4,2,1,0:T(8,128)(2,1)S(1)} copy-done((bf16[2,2,2,512,192]{3,4,2,1,0:T(8,128)(2,1)S(1)}, bf16[2,2,2,512,192]{3,4,2,1,0:T(8,128)(2,1)}, u32[]{:S(2)}) %copy-start) | copy-done | bytes 1572888
  1.4 0.0 copy-start.1
  1.4 0.7 copy-done.1
  2.1 71.5 %gather_sum_exchange.1 = (bf16[512,128]{1,0:T(8,128)(2,1)S(1)}, bf16[64,128,128]{2,1,0:T(8,128)(2,1)S(1)}, bf16[64,512,128]{2,1,0:T(8,128)(2,1)S(1)}) custom-call(s32[64]{0:T(128)S(1)} %copy-done.1, bf16[2,2,2,192,512]{4,3,2,1,0:T(8,128)(2,1)S(1)} %bitcast.2, bf16[2,2,2048,1024]{3,2,1,0:T(8,128)(2,1)} %leg_ref.1), custom_call_target="tpu_custom_call" | custom-call | tf_op jit(solution)/shard_map/gather_sum_exchange/pallas_call | solution.py:405
  73.6 3.7 %synthesis_product.1 = bf16[64,512,128]{2,1,0:T(8,128)(2,1)} custom-call(bf16[512,128]{1,0:T(8,128)(2,1)S(1)} %get-tuple-element.8.table_ref, bf16[64,128,128]{2,1,0:T(8,128)(2,1)S(1)} %get-tuple-element.9.wind_ref, bf16[64,512,128]{2,1,0:T(8,128)(2,1)S(1)} %get-tuple-element.10.vort_ref), custom_call_target="tpu_custom_call" | custom-call | tf_op jit(solution)/shard_map/synthesis_product/pallas_call | solution.py:443
Async XLA Ops:
  0.0 1.4 %copy-start = (bf16[2,2,2,512,192]{3,4,2,1,0:T(8,128)(2,1)S(1)}, bf16[2,2,2,512,192]{3,4,2,1,0:T(8,128)(2,1)}, u32[]{:S(2)}) copy-start(bf16[2,2,2,512,192]{3,4,2,1,0:T(8,128)(2,1)} %param.3) | copy-start | bytes 4718596
  1.4 0.7 copy-start.1
